TPU v7x, 32 devices: a whole 2x2x4 slice. The times are simulated.
32 devices in a mesh: tm: 16 (over z, x, core), mp: 2 (over y).
Axes of the slice: x: 2, y: 2, z: 4, core: 2. Of those that a mesh axis runs over, the one named last changes fastest.
Arguments:
- tokens: bfloat16 [4096, 1024], P('tm'), may hold values from -9 to 9
- norm1_gain: float32 [1024], replicated, may hold values from 0.5 to 1.5
- query_weight: bfloat16 [1024, 1024], P(None, 'mp'), may hold values from -1 to 1
- key_weight: bfloat16 [1024, 1024], P(None, 'mp'), may hold values from -1 to 1
- value_weight: bfloat16 [1024, 1024], P(None, 'mp'), may hold values from -0.1875 to 0.1875
- output_weight: bfloat16 [1024, 1024], P('mp'), may hold values from -5 to 5
- pattern: int32 [32, 8], replicated, may hold values from -1 to 31, as said below
- adjacency: int32 [128, 128], replicated, may hold values 0 or 1
- decay_rate: float32 [1024], P('mp'), may hold values from 0.015625 to 0.1
- norm2_gain: float32 [1024], replicated, may hold values from 0.5 to 1.5
- up_weight: bfloat16 [1024, 4096], P(None, 'mp'), may hold values from -0.1875 to 0.1875
- down_weight: bfloat16 [4096, 1024], P('mp'), may hold values from -0.09375 to 0.09375
Outputs:
- layer_out: bfloat16 [4096, 1024], P('tm', 'mp')
Inputs may be any that keep to these rules, and one draw needn't show every extreme that they name: pattern[b, 0] = b and pattern[b, 1] = b - 1. For the rows of the blocks g * 2 to g * 2 + 1, entry 2 + k (k from 0 to 5) is the same in all these rows: -1 where g < 2^k, else one of the blocks (g - 2^k) * 2 to (g - 2^k) * 2 + 1, never the block g * 2 - 1.
All inputs are finite; a program needn't handle non-finite values.
Results may differ from a plain program's by a relative error of at most 0.01.
Values may be sent and summed in bfloat16 or wider, within the bound.
A program may use at most 64 MiB of HBM per device.

v0:
```python
import math
import jax
import jax.numpy as jnp
from jax import lax
from jax.sharding import PartitionSpec as P

HD = 128


def from_behind(value, axis, steps):
    count = lax.axis_size(axis)
    first, last = (max(0, -steps), min(count, count - steps))
    return lax.ppermute(value, axis, [(source, source + steps) for source in range(first, last)])


def rms_norm(rows, gain):
    widened = rows.astype(jnp.float32)
    square = jnp.mean(widened * widened, axis=-1, keepdims=True)
    return (widened * lax.rsqrt(square + 1e-05) * gain).astype(jnp.bfloat16)


def block_partial(queries, key_rows, value_rows, heads):
    head_size = queries.shape[-1] // heads
    query_split = queries.reshape(queries.shape[:-1] + (heads, head_size))
    key_split = key_rows.reshape(key_rows.shape[:-1] + (heads, head_size))
    value_split = value_rows.reshape(value_rows.shape[:-1] + (heads, head_size))
    scores = jnp.einsum(
        "...qhd,...khd->...hqk", query_split, key_split, preferred_element_type=jnp.float32
    ) * (1.0 / math.sqrt(head_size))
    tops = jnp.max(scores, axis=-1)
    probs = jnp.exp(scores - tops[..., None])
    totals = jnp.sum(probs, axis=-1)
    weights = probs.astype(jnp.bfloat16)
    outputs = jnp.einsum(
        "...hqk,...khd->...qhd", weights, value_split, preferred_element_type=jnp.float32
    )
    return (tops, totals, outputs.reshape(outputs.shape[:-2] + (heads * head_size,)))


def merge_partials(tops, totals, outputs, valid, heads):
    flags = valid[..., None, None]
    masked = jnp.where(flags, tops, -jnp.inf)
    largest = jnp.max(masked, axis=-3)
    factor = jnp.where(flags, jnp.exp(jnp.where(flags, tops, 0.0) - largest[..., None, :, :]), 0.0)
    denom = jnp.sum(factor * totals, axis=-3)
    split = outputs.reshape(outputs.shape[:-1] + (heads, -1))
    numer = jnp.sum(jnp.swapaxes(factor, -1, -2)[..., None] * split, axis=-4)
    result = numer / jnp.swapaxes(denom, -1, -2)[..., None]
    return result.reshape(result.shape[:-2] + (-1,)).astype(jnp.bfloat16)


def running(frames, retain, inject):
    driven = frames.astype(jnp.float32) * inject
    factors = jnp.broadcast_to(retain, driven.shape)

    def join(earlier, later):
        return (earlier[0] * later[0], later[0] * earlier[1] + later[1])

    return lax.associative_scan(join, (factors, driven), axis=0)[1]


def per_device(
    tokens,
    norm1_gain,
    query_weight,
    key_weight,
    value_weight,
    output_weight,
    pattern,
    adjacency,
    decay_rate,
    norm2_gain,
    up_weight,
    down_weight,
):
    groups = lax.axis_size("tm")
    position = lax.axis_index("tm")
    width = query_weight.shape[1]
    heads = width // HD
    sites = adjacency.shape[0]
    steps = tokens.shape[0] // sites
    normed = rms_norm(tokens, norm1_gain)
    queries = (
        jnp.dot(normed, query_weight, preferred_element_type=jnp.float32)
        .astype(jnp.bfloat16)
        .reshape(steps, sites, width)
    )
    key_rows = jnp.dot(normed, key_weight, preferred_element_type=jnp.float32).astype(jnp.bfloat16)
    value_rows = jnp.dot(normed, value_weight, preferred_element_type=jnp.float32).astype(
        jnp.bfloat16
    )
    key_blocks = key_rows.reshape(steps, sites, width)
    value_blocks = value_rows.reshape(steps, sites, width)
    own_entries = lax.dynamic_slice_in_dim(pattern, position * steps, steps, 0)
    remote = own_entries[:, 2:]
    far_count = remote.shape[1]
    key_last, value_last = from_behind((key_blocks[steps - 1], value_blocks[steps - 1]), "tm", 1)
    prior_keys = jnp.concatenate([key_last[None], key_blocks[:-1]], axis=0)
    prior_values = jnp.concatenate([value_last[None], value_blocks[:-1]], axis=0)
    self_part = block_partial(queries, key_blocks, value_blocks, heads)
    prior_part = block_partial(queries, prior_keys, prior_values, heads)
    spread_queries = jnp.broadcast_to(queries[:, None], (steps, far_count, sites, width))
    wanted = pattern[:, 2:].reshape(groups, -1)
    local_pick = wanted - position * steps
    hits = (wanted >= 0) & (local_pick >= 0) & (local_pick < steps)
    selector = jnp.any(
        (local_pick[:, :, None] == jnp.arange(steps, dtype=jnp.int32)[None, None, :])
        & hits[:, :, None],
        axis=1,
    ).astype(jnp.bfloat16)
    send_keys = jnp.einsum(
        "gs,sbf->gbf", selector, key_blocks, preferred_element_type=jnp.float32
    ).astype(jnp.bfloat16)
    send_values = jnp.einsum(
        "gs,sbf->gbf", selector, value_blocks, preferred_element_type=jnp.float32
    ).astype(jnp.bfloat16)
    got_keys, got_values = (
        lax.all_to_all(send_keys, "tm", split_axis=0, concat_axis=0, tiled=True),
        lax.all_to_all(send_values, "tm", split_axis=0, concat_axis=0, tiled=True),
    )
    source = jnp.maximum(remote, 0) // steps
    far_part = block_partial(spread_queries, got_keys[source], got_values[source], heads)
    tops = jnp.concatenate([self_part[0][:, None], prior_part[0][:, None], far_part[0]], axis=1)
    totals = jnp.concatenate([self_part[1][:, None], prior_part[1][:, None], far_part[1]], axis=1)
    outputs = jnp.concatenate([self_part[2][:, None], prior_part[2][:, None], far_part[2]], axis=1)
    block_ids = position * steps + jnp.arange(steps, dtype=jnp.int32)
    valid = jnp.concatenate(
        [jnp.ones((steps, 1), bool), (block_ids > 0)[:, None], remote >= 0], axis=1
    )
    attended = merge_partials(tops, totals, outputs, valid, heads).reshape(steps * sites, width)
    projected = lax.psum_scatter(
        jnp.dot(attended, output_weight, preferred_element_type=jnp.float32),
        "mp",
        scatter_dimension=1,
        tiled=True,
    )
    columns = projected.shape[1]
    own_tokens = lax.dynamic_slice_in_dim(tokens, lax.axis_index("mp") * columns, columns, 1)
    first = (own_tokens.astype(jnp.float32) + projected).astype(jnp.bfloat16)
    links = jnp.maximum(adjacency, jnp.eye(sites, dtype=jnp.int32))
    degree = jnp.sum(links, axis=1).astype(jnp.float32)
    grid = first.reshape(steps, sites, columns)
    mixed = (
        jnp.einsum(
            "st,btc->bsc", links.astype(jnp.bfloat16), grid, preferred_element_type=jnp.float32
        )
        / degree[None, :, None]
    ).astype(jnp.bfloat16)
    retain = jnp.exp(-decay_rate)
    inject = jnp.sqrt(1.0 - retain * retain)
    by_site = lax.all_to_all(mixed, "tm", split_axis=1, concat_axis=0, tiled=True)
    states = running(by_site, retain, inject).astype(jnp.bfloat16)
    smoothed = lax.all_to_all(states, "tm", split_axis=0, concat_axis=1, tiled=True)
    second = (
        first.astype(jnp.float32) + smoothed.reshape(steps * sites, columns).astype(jnp.float32)
    ).astype(jnp.bfloat16)
    whole = lax.all_gather(second, "mp", axis=1, tiled=True)
    normed_late = rms_norm(whole, norm2_gain)
    hidden = jax.nn.gelu(
        jnp.dot(normed_late, up_weight, preferred_element_type=jnp.float32), approximate=True
    ).astype(jnp.bfloat16)
    summed = lax.psum_scatter(
        jnp.dot(hidden, down_weight, preferred_element_type=jnp.float32),
        "mp",
        scatter_dimension=1,
        tiled=True,
    )
    return (second.astype(jnp.float32) + summed).astype(jnp.bfloat16)


def solution(mesh):
    placed = (
        P("tm", None),
        P(),
        P(None, "mp"),
        P(None, "mp"),
        P(None, "mp"),
        P("mp", None),
        P(),
        P(),
        P("mp"),
        P(),
        P(None, "mp"),
        P("mp", None),
    )
    return jax.shard_map(
        per_device, mesh=mesh, in_specs=placed, out_specs=P("tm", "mp"), check_vma=False
    )
```

profile of v0, /device:TPU:0, one launch (start us, length us, event | category | flops | bytes accessed | tf_op | source)
XLA Modules:
  0.0 243.4 jit_solution(6739945608081619143)
XLA Ops:
  6.5 1.3 fusion.16
  7.9 0.7 slice_compare_fusion
  9.7 1.9 convolution_convert_fusion.2
  11.6 0.8 convolution_convert_fusion
  12.4 2.5 %copy.148 = bf16[16,128,512]{2,1,0:T(8,128)(2,1)} copy(bf16[16,128,512]{2,0,1:T(8,128)(2,1)S(1)} %convolution_convert_fusion) | data formatting | bytes 4194304 | tf_op jit(solution)/shard_map/convert_element_type | solution.py:116
  15.0 7.5 %all-to-all-start.1 = ((bf16[16,128,512]{2,1,0:T(8,128)(2,1)}), bf16[16,128,512]{2,1,0:T(8,128)(2,1)S(1)}, u32[]{:S(2)}, u32[]{:S(2)}) async-start(bf16[16,128,512]{2,1,0:T(8,128)(2,1)} %copy.148), calls=%async_computation.1 | async-start | bytes 4194304 | tf_op jit(solution)/shard_map/all_to_all | solution.py:119
  22.5 1.9 convolution_convert_fusion.3
  24.4 0.7 copy-done.2
  25.1 0.8 convolution_convert_fusion.1
  25.9 2.5 %copy.138 = bf16[16,128,512]{2,1,0:T(8,128)(2,1)} copy(bf16[16,128,512]{2,0,1:T(8,128)(2,1)S(1)} %convolution_convert_fusion.1) | data formatting | bytes 4194304 | tf_op jit(solution)/shard_map/convert_element_type | solution.py:113
  28.3 35.2 %all-to-all-done.1 = bf16[16,128,512]{2,1,0:T(8,128)(2,1)S(1)} async-done(((bf16[16,128,512]{2,1,0:T(8,128)(2,1)}), bf16[16,128,512]{2,1,0:T(8,128)(2,1)S(1)}, u32[]{:S(2)}, u32[]{:S(2)}) %all-to-all-start.1) | async-done | bytes 2097184 | tf_op jit(solution)/shard_map/all_to_all | solution.py:119
  63.6 11.3 %all-to-all-start = ((bf16[16,128,512]{2,1,0:T(8,128)(2,1)}), bf16[16,128,512]{2,1,0:T(8,128)(2,1)}, u32[]{:S(2)}, u32[]{:S(2)}) async-start(bf16[16,128,512]{2,1,0:T(8,128)(2,1)} %copy.138), calls=%async_computation | async-start | bytes 4194304 | tf_op jit(solution)/shard_map/all_to_all | solution.py:118
  74.9 1.7 fusion.94
  76.6 2.9 %collective-permute-start = (bf16[128,512]{1,0:T(8,128)(2,1)}, bf16[128,512]{1,0:T(8,128)(2,1)}, u32[]{:S(2)}, u32[]{:S(2)}) collective-permute-start(bf16[128,512]{1,0:T(8,128)(2,1)} %get-tuple-element.7), channel_id=1, source_target_pairs={{0,2},{2,4},{4,6},{6,8},{8,10},{10,12},{12,14},{14,16},{16,18},{18... | collective-permute-start | bytes 393224 | tf_op jit(solution)/shard_map/ppermute | solution.py:13
  79.5 0.7 fusion.93
  80.2 3.5 %collective-permute-start.1 = (bf16[128,512]{1,0:T(8,128)(2,1)}, bf16[128,512]{1,0:T(8,128)(2,1)}, u32[]{:S(2)}, u32[]{:S(2)}) collective-permute-start(bf16[128,512]{1,0:T(8,128)(2,1)} %get-tuple-element.5), channel_id=1, source_target_pairs={{0,2},{2,4},{4,6},{6,8},{8,10},{10,12},{12,14},{14,16},{16,18},{18... | collective-permute-start | bytes 393224 | tf_op jit(solution)/shard_map/ppermute | solution.py:13
  83.8 1.7 reshape_reshape.11
  85.5 0.8 reshape_reshape.12
  86.5 2.6 %convolution_convert_fusion.4 = bf16[256,512]{1,0:T(8,128)(2,1)} fusion(bf16[1024,512]{1,0:T(8,128)(2,1)} %param.14, bf16[256,1024]{1,0:T(8,128)(2,1)} %param.12, f32[1024]{0:T(1024)S(1)} %copy-done.11, f32[256]{0:T(256)S(1)} %add_rsqrt_fusion.1), kind=kOutput, calls=%fused_computation.34 | convolution fusion | flops 269615104 | bytes 1840128 | tf_op jit(solution)/shard_map/dot_general | solution.py:84
  89.1 1.0 reshape_reshape.10
  90.1 0.7 copy.129
  90.8 0.9 concatenate.47
  92.4 1.0 copy.165
  94.2 1.3 fusion.97
  95.4 2.0 convolution_bitcast_fusion.2
  97.6 1.6 concatenate.46
  99.2 1.6 copy.131
  100.7 1.7 copy.164
  102.4 1.3 fusion.96
  103.8 2.0 convolution_bitcast_fusion.1
  105.7 1.9 gather_fusion.1
  107.6 2.6 %copy.149 = bf16[12,128,512]{1,2,0:T(8,128)(2,1)} copy(bf16[12,128,512]{2,1,0:T(8,128)(2,1)} %gather_fusion.1) | data formatting | bytes 3145728 | tf_op jit(solution)/shard_map/gather | solution.py:122
  110.2 5.8 %all-to-all-done = bf16[16,128,512]{2,1,0:T(8,128)(2,1)} async-done(((bf16[16,128,512]{2,1,0:T(8,128)(2,1)}), bf16[16,128,512]{2,1,0:T(8,128)(2,1)}, u32[]{:S(2)}, u32[]{:S(2)}) %all-to-all-start) | async-done | bytes 2097184 | tf_op jit(solution)/shard_map/all_to_all | solution.py:118
  116.0 3.4 %gather_fusion = bf16[12,128,512]{2,1,0:T(8,128)(2,1)} fusion(bf16[16,128,512]{2,1,0:T(8,128)(2,1)} %all-to-all-done, s32[1024]{0:T(1024)S(1)} %pad_clamp_fusion), kind=kCustom, calls=%fused_computation | custom fusion | bytes 3145776 | tf_op jit(solution)/shard_map/gather | solution.py:122
  119.4 1.9 copy.140
  121.4 1.3 multiply_reduce_fusion
  123.4 0.7 copy-done.1
  126.1 1.4 fusion.47
  127.7 40.5 %reduce-scatter.3.cloned.1.call-done = f32[256,512]{1,0:T(8,128)} async-done(((f32[256,1024]{1,0:T(8,128)}), f32[256,512]{1,0:T(8,128)}) %reduce-scatter.3.cloned.1.call-update) | async-done | bytes 524304 | tf_op jit(solution)/shard_map/reduce_scatter | solution.py:131
  168.2 1.1 add_convert_fusion.2
  169.6 0.9 copy.155
  170.5 5.6 %all-to-all-start.2 = ((bf16[2,128,512]{2,0,1:T(2,128)(2,1)}), bf16[2,128,512]{2,0,1:T(2,128)(2,1)S(1)}, u32[]{:S(2)}, u32[]{:S(2)}) async-start(bf16[2,128,512]{2,0,1:T(2,128)(2,1)} %copy.155), calls=%async_computation.3 | async-start | bytes 524288 | tf_op jit(solution)/shard_map/all_to_all | solution.py:151
  176.1 10.0 %all-to-all-done.2 = bf16[2,128,512]{2,0,1:T(2,128)(2,1)S(1)} async-done(((bf16[2,128,512]{2,0,1:T(2,128)(2,1)}), bf16[2,128,512]{2,0,1:T(2,128)(2,1)S(1)}, u32[]{:S(2)}, u32[]{:S(2)}) %all-to-all-start.2) | async-done | bytes 262176 | tf_op jit(solution)/shard_map/all_to_all | solution.py:151
  187.5 12.8 %all_to_all.28 = bf16[32,8,512]{2,1,0:T(8,128)(2,1)S(1)} all-to-all(bf16[32,8,512]{2,1,0:T(8,128)(2,1)S(1)} %add_convert_fusion.1), channel_id=1, replica_groups=mesh['tm'=16,'mp'=2] {'tm'}, dimensions={0} | all-to-all | bytes 524288 | tf_op jit(solution)/shard_map/all_to_all | solution.py:153
  200.5 8.7 %all_gather.3 = bf16[256,1024]{1,0:T(8,128)(2,1)S(1)} all-gather(bf16[256,512]{1,0:T(8,128)(2,1)S(1)} %fusion.36), channel_id=1, replica_groups=mesh['tm'=16,'mp'=2] {'mp'}, dimensions={1}, use_global_device_ids=true | all-gather | bytes 786432 | tf_op jit(solution)/shard_map/all_gather | solution.py:157
  209.5 7.1 %fusion.22 = f32[256,1024]{1,0:T(8,128)} fusion(bf16[2048,1024]{1,0:T(8,128)(2,1)} %param.23, bf16[1024,2048]{1,0:T(8,128)(2,1)} %param.22, bf16[256,1024]{1,0:T(8,128)(2,1)S(1)} %all_gather.3, f32[1024]{0:T(1024)S(1)} %copy-done.12, f32[256]{0:T(256)S(1)} %add_rsqrt_fusion), kind=kOutput, calls=%fused_computation.42 | convolution fusion | flops 2153250816 | bytes 9966592 | tf_op jit(solution)/shard_map/dot_general | solution.py:163
  216.6 18.1 %reduce-scatter.5.cloned.1.call-done = f32[256,512]{1,0:T(8,128)} async-done(((f32[256,1024]{1,0:T(8,128)}), f32[256,512]{1,0:T(8,128)}) %reduce-scatter.5.cloned.1.call-update) | async-done | bytes 524304 | tf_op jit(solution)/shard_map/reduce_scatter | solution.py:162
  234.8 1.8 add_convert_fusion
  (99 shorter events, 7.6 us)
Async XLA Ops:
  6.5 119.5 %copy-start = (bf16[512,1024]{1,0:T(8,128)(2,1)S(1)}, bf16[512,1024]{1,0:T(8,128)(2,1)}, u32[]{:S(2)}) copy-start(bf16[512,1024]{1,0:T(8,128)(2,1)} %param.17) | copy-start | bytes 3145732
  15.0 7.5 %copy-start.11 = (f32[1024]{0:T(1024)S(1)}, f32[1024]{0:T(1024)}, u32[]{:S(2)}) copy-start(f32[1024]{0:T(1024)} %param.13) | copy-start | bytes 12292
  15.0 48.6 %all-to-all-start.1 = ((bf16[16,128,512]{2,1,0:T(8,128)(2,1)}), bf16[16,128,512]{2,1,0:T(8,128)(2,1)S(1)}, u32[]{:S(2)}, u32[]{:S(2)}) async-start(bf16[16,128,512]{2,1,0:T(8,128)(2,1)} %copy.148), calls=%async_computation.1 | async-start | bytes 4194304 | tf_op jit(solution)/shard_map/all_to_all | solution.py:119
  24.4 0.7 copy-start.2
  63.6 52.4 %all-to-all-start = ((bf16[16,128,512]{2,1,0:T(8,128)(2,1)}), bf16[16,128,512]{2,1,0:T(8,128)(2,1)}, u32[]{:S(2)}, u32[]{:S(2)}) async-start(bf16[16,128,512]{2,1,0:T(8,128)(2,1)} %copy.138), calls=%async_computation | async-start | bytes 4194304 | tf_op jit(solution)/shard_map/all_to_all | solution.py:118
  74.8 11.4 %copy-start.8 = (s32[32,8]{0,1:T(8,128)S(1)}, s32[32,8]{0,1:T(8,128)}, u32[]{:S(2)}) copy-start(s32[32,8]{0,1:T(8,128)} %param.18) | copy-start | bytes 3076
  74.9 93.3 %reduce-scatter.3.cloned.1.call-start = ((), (), s32[]{:S(2)}) async-start(), calls=%async_computation.6 | async-start | bytes 1572864 | tf_op jit(solution)/shard_map/reduce_scatter | solution.py:131
  76.6 21.0 %collective-permute-start = (bf16[128,512]{1,0:T(8,128)(2,1)}, bf16[128,512]{1,0:T(8,128)(2,1)}, u32[]{:S(2)}, u32[]{:S(2)}) collective-permute-start(bf16[128,512]{1,0:T(8,128)(2,1)} %get-tuple-element.7), channel_id=1, source_target_pairs={{0,2},{2,4},{4,6},{6,8},{8,10},{10,12},{12,14},{14,16},{16,18},{18... | collective-permute-start | bytes 393224 | tf_op jit(solution)/shard_map/ppermute | solution.py:13
  80.2 20.5 %collective-permute-start.1 = (bf16[128,512]{1,0:T(8,128)(2,1)}, bf16[128,512]{1,0:T(8,128)(2,1)}, u32[]{:S(2)}, u32[]{:S(2)}) collective-permute-start(bf16[128,512]{1,0:T(8,128)(2,1)} %get-tuple-element.5), channel_id=1, source_target_pairs={{0,2},{2,4},{4,6},{6,8},{8,10},{10,12},{12,14},{14,16},{16,18},{18... | collective-permute-start | bytes 393224 | tf_op jit(solution)/shard_map/ppermute | solution.py:13
  119.4 2.0 copy-start.6
  122.7 1.4 copy-start.1
  124.1 0.7 copy-start.9
  124.1 1.0 copy-start.3
  124.1 1.2 copy-start.4
  125.8 1.7 copy-start.7
  125.9 42.3 %copy-start.5 = (bf16[256,1024]{1,0:T(8,128)(2,1)S(1)}, bf16[256,1024]{1,0:T(8,128)(2,1)}, u32[]{:S(2)}) copy-start(bf16[256,1024]{1,0:T(8,128)(2,1)} %param.12) | copy-start | bytes 1572868
  127.5 48.6 %copy-start.10 = (f32[512]{0:T(512)S(1)}, f32[512]{0:T(512)}, u32[]{:S(2)}) copy-start(f32[512]{0:T(512)} %param.20) | copy-start | bytes 6148
  170.5 15.7 %all-to-all-start.2 = ((bf16[2,128,512]{2,0,1:T(2,128)(2,1)}), bf16[2,128,512]{2,0,1:T(2,128)(2,1)S(1)}, u32[]{:S(2)}, u32[]{:S(2)}) async-start(bf16[2,128,512]{2,0,1:T(2,128)(2,1)} %copy.155), calls=%async_computation.3 | async-start | bytes 524288 | tf_op jit(solution)/shard_map/all_to_all | solution.py:151
  176.1 58.7 %reduce-scatter.5.cloned.1.call-start = ((), (), s32[]{:S(2)}) async-start(), calls=%async_computation.7 | async-start | bytes 1572864 | tf_op jit(solution)/shard_map/reduce_scatter | solution.py:162
  200.3 9.1 %copy-start.12 = (f32[1024]{0:T(1024)S(1)}, f32[1024]{0:T(1024)}, u32[]{:S(2)}) copy-start(f32[1024]{0:T(1024)} %param.21) | copy-start | bytes 12292
Sparse Core Ops, SparseCore 0:
  127.7 40.4 reduce-scatter.2
  216.7 17.9 reduce-scatter.4
where the time goes:
time: 244 us; the launch traced here: 243 us
  waiting for transfers between devices  110 us (45%)
  local copies, waits for them, and re-layouts  33.6 us (14%)
  starting transfers between devices  30.9 us (13%)
  matrix products  25.2 us (10%)
  blocking collectives  21.6 us (9%)
  between operations  14 us (6%)
  other arithmetic  8.48 us (3%)
    reduce_scatter x1, waiting for transfers between devices, per_device(): lax.psum_scatter(jnp.dot(attended, output_weight, preferred_element_type=...  40.5 us
    all_to_all x1, waiting for transfers between devices, per_device(): lax.all_to_all(send_values, 'tm', split_axis=0, concat_axis=0, tiled=True)  35.2 us
    reduce_scatter x1, waiting for transfers between devices, per_device(): lax.psum_scatter(jnp.dot(hidden, down_weight, preferred_element_type=jnp....  18.1 us
    all_to_all x1, blocking collectives, per_device(): lax.all_to_all(states, 'tm', split_axis=0, concat_axis=1, tiled=True)  12.8 us
    all_to_all x1, starting transfers between devices, per_device(): lax.all_to_all(send_keys, 'tm', split_axis=0, concat_axis=0, tiled=True)  11.3 us
    all_to_all x1, waiting for transfers between devices, per_device(): lax.all_to_all(mixed, 'tm', split_axis=1, concat_axis=0, tiled=True)  9.97 us
    all_gather x1, blocking collectives, per_device(): whole = lax.all_gather(second, 'mp', axis=1, tiled=True)  8.75 us
    all_to_all x1, starting transfers between devices, per_device(): lax.all_to_all(send_values, 'tm', split_axis=0, concat_axis=0, tiled=True)  7.49 us
  transfers between devices with their start and end apart: 7, of which 5 were waited for; matrix products, arithmetic and copies ran while one was open for 14% of the time, Pallas kernels for 0%

commit v1 on v0

--- a/solution.py
+++ b/solution.py
@@ -5,6 +5,23 @@
 from jax.sharding import PartitionSpec as P
 
 HD = 128
+
+
+def run_the_tiles(work_x):
+    block_out, p_next = (lax.axis_size("tm"), lax.axis_index("tm"))
+    opened = work_x.shape[0] // block_out
+    a_now = jnp.roll(work_x, -p_next * opened, axis=0)
+    tray = [lax.slice_in_dim(a_now, 0, opened, axis=0)]
+    for ii in range(1, block_out):
+        next_value = lax.slice_in_dim(a_now, ii * opened, (ii + 1) * opened, axis=0)
+        tray.append(
+            lax.ppermute(
+                next_value, "tm", [(idx, (idx + ii) % block_out) for idx in range(block_out)]
+            )
+        )
+    v1 = jnp.concatenate(tray[::-1], axis=1)
+    now = jnp.roll(v1, (p_next + 1) * tray[0].shape[1], axis=1)
+    return now
 
 
 def from_behind(value, axis, steps):
@@ -150,7 +167,7 @@
     inject = jnp.sqrt(1.0 - retain * retain)
     by_site = lax.all_to_all(mixed, "tm", split_axis=1, concat_axis=0, tiled=True)
     states = running(by_site, retain, inject).astype(jnp.bfloat16)
-    smoothed = lax.all_to_all(states, "tm", split_axis=0, concat_axis=1, tiled=True)
+    smoothed = run_the_tiles(states)
     second = (
         first.astype(jnp.float32) + smoothed.reshape(steps * sites, columns).astype(jnp.float32)
     ).astype(jnp.bfloat16)

time: 244 us -> 255 us (1.045)
  starting transfers between devices: 30.9 us -> 49.7 us
  blocking collectives: 21.6 us -> 7.27 us
  waiting for transfers between devices: 110 us -> 115 us
    ppermute x0 -> x15, starting transfers between devices: none -> 18.8 us  [run_the_tiles(): lax.ppermute(next_value, 'tm', [(idx, (idx + ii) % block_out) for idx in...]
    all_to_all x1 -> x0, blocking collectives: 12.8 us -> none  [per_device(): lax.all_to_all(states, 'tm', split_axis=0, concat_axis=1, tiled=True)]
    ppermute x0 -> x15, waiting for transfers between devices: none -> 5.83 us  [run_the_tiles(): lax.ppermute(next_value, 'tm', [(idx, (idx + ii) % block_out) for idx in...]
  transfers between devices with their start and end apart: 7 -> 22, of which waited for: 5 -> 8; matrix products, arithmetic and copies ran while one was open for 14% -> 13% of each run, Pallas kernels for 0% -> 0%
where the time goes in v1:
time: 255 us; the launch traced here: 254 us
  waiting for transfers between devices  115 us (45%)
  starting transfers between devices  49.7 us (19%)
  local copies, waits for them, and re-layouts  33.8 us (13%)
  matrix products  25.2 us (10%)
  between operations  14.2 us (6%)
  other arithmetic  8.69 us (3%)
  blocking collectives  7.27 us (3%)
    reduce_scatter x1, waiting for transfers between devices, per_device(): lax.psum_scatter(jnp.dot(attended, output_weight, preferred_element_type=...  40.5 us
    all_to_all x1, waiting for transfers between devices, per_device(): lax.all_to_all(send_values, 'tm', split_axis=0, concat_axis=0, tiled=True)  35.2 us
    ppermute x15, starting transfers between devices, run_the_tiles(): lax.ppermute(next_value, 'tm', [(idx, (idx + ii) % block_out) for idx in...  18.8 us
    reduce_scatter x1, waiting for transfers between devices, per_device(): lax.psum_scatter(jnp.dot(hidden, down_weight, preferred_element_type=jnp....  17.9 us
    all_to_all x1, starting transfers between devices, per_device(): lax.all_to_all(send_keys, 'tm', split_axis=0, concat_axis=0, tiled=True)  11.3 us
    all_to_all x1, waiting for transfers between devices, per_device(): lax.all_to_all(mixed, 'tm', split_axis=1, concat_axis=0, tiled=True)  9.94 us
    all_to_all x1, starting transfers between devices, per_device(): lax.all_to_all(send_values, 'tm', split_axis=0, concat_axis=0, tiled=True)  7.49 us
    all_gather x1, blocking collectives, per_device(): whole = lax.all_gather(second, 'mp', axis=1, tiled=True)  7.27 us
  transfers between devices with their start and end apart: 22, of which 8 were waited for; matrix products, arithmetic and copies ran while one was open for 13% of the time, Pallas kernels for 0%

profile of v1, /device:TPU:0, one launch (start us, length us, event | category | flops | bytes accessed | tf_op | source)
XLA Modules:
  0.0 253.9 jit_solution(1273020102757085261)
XLA Ops:
  6.5 1.3 fusion.16
  9.7 1.9 convolution_convert_fusion.2
  12.4 2.5 copy.175
  15.0 7.5 %all-to-all-start.1 = ((bf16[16,128,512]{2,1,0:T(8,128)(2,1)}), bf16[16,128,512]{2,1,0:T(8,128)(2,1)S(1)}, u32[]{:S(2)}, u32[]{:S(2)}) async-start(bf16[16,128,512]{2,1,0:T(8,128)(2,1)} %copy.175), calls=%async_computation.1 | async-start | bytes 4194304 | tf_op jit(solution)/shard_map/all_to_all | solution.py:136
  22.5 1.9 convolution_convert_fusion.3
  25.9 2.5 copy.165
  28.3 35.2 %all-to-all-done.1 = bf16[16,128,512]{2,1,0:T(8,128)(2,1)S(1)} async-done(((bf16[16,128,512]{2,1,0:T(8,128)(2,1)}), bf16[16,128,512]{2,1,0:T(8,128)(2,1)S(1)}, u32[]{:S(2)}, u32[]{:S(2)}) %all-to-all-start.1) | async-done | bytes 2097184 | tf_op jit(solution)/shard_map/all_to_all | solution.py:136
  63.6 11.3 %all-to-all-start = ((bf16[16,128,512]{2,1,0:T(8,128)(2,1)}), bf16[16,128,512]{2,1,0:T(8,128)(2,1)}, u32[]{:S(2)}, u32[]{:S(2)}) async-start(bf16[16,128,512]{2,1,0:T(8,128)(2,1)} %copy.165), calls=%async_computation | async-start | bytes 4194304 | tf_op jit(solution)/shard_map/all_to_all | solution.py:135
  74.9 1.7 fusion.96
  76.6 2.9 %collective-permute-start = (bf16[128,512]{1,0:T(8,128)(2,1)}, bf16[128,512]{1,0:T(8,128)(2,1)}, u32[]{:S(2)}, u32[]{:S(2)}) collective-permute-start(bf16[128,512]{1,0:T(8,128)(2,1)} %get-tuple-element.22), channel_id=1, source_target_pairs={{0,2},{2,4},{4,6},{6,8},{8,10},{10,12},{12,14},{14,16},{16,18},{18... | collective-permute-start | bytes 393224 | tf_op jit(solution)/shard_map/ppermute | solution.py:30
  80.2 3.5 %collective-permute-start.1 = (bf16[128,512]{1,0:T(8,128)(2,1)}, bf16[128,512]{1,0:T(8,128)(2,1)}, u32[]{:S(2)}, u32[]{:S(2)}) collective-permute-start(bf16[128,512]{1,0:T(8,128)(2,1)} %get-tuple-element.20), channel_id=1, source_target_pairs={{0,2},{2,4},{4,6},{6,8},{8,10},{10,12},{12,14},{14,16},{16,18},{18... | collective-permute-start | bytes 393224 | tf_op jit(solution)/shard_map/ppermute | solution.py:30
  83.8 1.7 reshape_reshape.11
  86.5 2.6 %convolution_convert_fusion.4 = bf16[256,512]{1,0:T(8,128)(2,1)} fusion(bf16[1024,512]{1,0:T(8,128)(2,1)} %param.14, bf16[256,1024]{1,0:T(8,128)(2,1)} %param.12, f32[1024]{0:T(1024)S(1)} %copy-done.11, f32[256]{0:T(256)S(1)} %add_rsqrt_fusion.1), kind=kOutput, calls=%fused_computation.34 | convolution fusion | flops 269615104 | bytes 1840128 | tf_op jit(solution)/shard_map/dot_general | solution.py:101
  92.5 1.0 copy.191
  94.3 1.3 fusion.99
  95.5 2.0 convolution_bitcast_fusion.2
  97.7 1.6 concatenate.56
  99.2 1.6 copy.158
  100.8 1.7 copy.190
  102.5 1.3 fusion.98
  103.9 2.0 convolution_bitcast_fusion.1
  105.8 1.9 gather_fusion.1
  107.7 2.6 %copy.176 = bf16[12,128,512]{1,2,0:T(8,128)(2,1)} copy(bf16[12,128,512]{2,1,0:T(8,128)(2,1)} %gather_fusion.1) | data formatting | bytes 3145728 | tf_op jit(solution)/shard_map/gather | solution.py:139
  110.3 5.7 %all-to-all-done = bf16[16,128,512]{2,1,0:T(8,128)(2,1)} async-done(((bf16[16,128,512]{2,1,0:T(8,128)(2,1)}), bf16[16,128,512]{2,1,0:T(8,128)(2,1)}, u32[]{:S(2)}, u32[]{:S(2)}) %all-to-all-start) | async-done | bytes 2097184 | tf_op jit(solution)/shard_map/all_to_all | solution.py:135
  116.0 3.4 %gather_fusion = bf16[12,128,512]{2,1,0:T(8,128)(2,1)} fusion(bf16[16,128,512]{2,1,0:T(8,128)(2,1)} %all-to-all-done, s32[1024]{0:T(1024)S(1)} %pad_clamp_fusion), kind=kCustom, calls=%fused_computation | custom fusion | bytes 3145776 | tf_op jit(solution)/shard_map/gather | solution.py:139
  119.4 1.9 copy.167
  121.4 1.3 multiply_reduce_fusion
  126.1 1.4 fusion.48
  127.7 40.5 %reduce-scatter.3.cloned.1.call-done = f32[256,512]{1,0:T(8,128)} async-done(((f32[256,1024]{1,0:T(8,128)}), f32[256,512]{1,0:T(8,128)}) %reduce-scatter.3.cloned.1.call-update) | async-done | bytes 524304 | tf_op jit(solution)/shard_map/reduce_scatter | solution.py:148
  168.1 1.1 add_convert_fusion.2
  170.4 5.6 %all-to-all-start.2 = ((bf16[2,128,512]{2,0,1:T(2,128)(2,1)}), bf16[2,128,512]{2,0,1:T(2,128)(2,1)S(1)}, u32[]{:S(2)}, u32[]{:S(2)}) async-start(bf16[2,128,512]{2,0,1:T(2,128)(2,1)} %copy.182), calls=%async_computation.3 | async-start | bytes 524288 | tf_op jit(solution)/shard_map/all_to_all | solution.py:168
  176.1 9.9 %all-to-all-done.2 = bf16[2,128,512]{2,0,1:T(2,128)(2,1)S(1)} async-done(((bf16[2,128,512]{2,0,1:T(2,128)(2,1)}), bf16[2,128,512]{2,0,1:T(2,128)(2,1)S(1)}, u32[]{:S(2)}, u32[]{:S(2)}) %all-to-all-start.2) | async-done | bytes 262176 | tf_op jit(solution)/shard_map/all_to_all | solution.py:168
  187.7 1.4 collective-permute-start.2
  189.2 1.0 collective-permute-start.3
  191.1 2.0 collective-permute-start.6
  193.1 1.6 collective-permute-start.7
  195.0 2.1 collective-permute-start.9
  197.1 2.3 collective-permute-start.10
  199.4 1.5 collective-permute-start.11
  201.0 2.2 collective-permute-start.13
  203.3 2.1 collective-permute-start.14
  205.3 1.2 collective-permute-start.15
  206.6 1.8 collective-permute-done.14
  208.5 3.3 %collective-permute-done.15 = bf16[2,8,512]{2,1,0:T(8,128)(2,1)S(1)} collective-permute-done((bf16[2,8,512]{2,1,0:T(8,128)(2,1)S(1)}, bf16[2,8,512]{2,1,0:T(8,128)(2,1)S(1)}, u32[]{:S(2)}, u32[]{:S(2)}) %collective-permute-start.15) | collective-permute-done | bytes 16416 | tf_op jit(solution)/shard_map/ppermute | solution.py:18
  212.7 7.3 %all_gather.3 = bf16[256,1024]{1,0:T(8,128)(2,1)S(1)} all-gather(bf16[256,512]{1,0:T(8,128)(2,1)S(1)} %fusion.36), channel_id=1, replica_groups=mesh['tm'=16,'mp'=2] {'mp'}, dimensions={1}, use_global_device_ids=true | all-gather | bytes 786432 | tf_op jit(solution)/shard_map/all_gather | solution.py:174
  220.2 7.1 %fusion.22 = f32[256,1024]{1,0:T(8,128)} fusion(bf16[2048,1024]{1,0:T(8,128)(2,1)} %param.23, bf16[1024,2048]{1,0:T(8,128)(2,1)} %param.22, bf16[256,1024]{1,0:T(8,128)(2,1)S(1)} %all_gather.3, f32[1024]{0:T(1024)S(1)} %copy-done.12, f32[256]{0:T(256)S(1)} %add_rsqrt_fusion), kind=kOutput, calls=%fused_computation.42 | convolution fusion | flops 2153250816 | bytes 9966592 | tf_op jit(solution)/shard_map/dot_general | solution.py:180
  227.3 17.9 %reduce-scatter.5.cloned.1.call-done = f32[256,512]{1,0:T(8,128)} async-done(((f32[256,1024]{1,0:T(8,128)}), f32[256,512]{1,0:T(8,128)}) %reduce-scatter.5.cloned.1.call-update) | async-done | bytes 524304 | tf_op jit(solution)/shard_map/reduce_scatter | solution.py:179
  245.3 1.8 add_convert_fusion
  (161 shorter events, 18.8 us)
Async XLA Ops:
  6.5 119.5 %copy-start = (bf16[512,1024]{1,0:T(8,128)(2,1)S(1)}, bf16[512,1024]{1,0:T(8,128)(2,1)}, u32[]{:S(2)}) copy-start(bf16[512,1024]{1,0:T(8,128)(2,1)} %param.17) | copy-start | bytes 3145732
  15.0 7.5 %copy-start.11 = (f32[1024]{0:T(1024)S(1)}, f32[1024]{0:T(1024)}, u32[]{:S(2)}) copy-start(f32[1024]{0:T(1024)} %param.13) | copy-start | bytes 12292
  15.0 48.6 %all-to-all-start.1 = ((bf16[16,128,512]{2,1,0:T(8,128)(2,1)}), bf16[16,128,512]{2,1,0:T(8,128)(2,1)S(1)}, u32[]{:S(2)}, u32[]{:S(2)}) async-start(bf16[16,128,512]{2,1,0:T(8,128)(2,1)} %copy.175), calls=%async_computation.1 | async-start | bytes 4194304 | tf_op jit(solution)/shard_map/all_to_all | solution.py:136
  24.4 0.7 copy-start.2
  63.6 52.4 %all-to-all-start = ((bf16[16,128,512]{2,1,0:T(8,128)(2,1)}), bf16[16,128,512]{2,1,0:T(8,128)(2,1)}, u32[]{:S(2)}, u32[]{:S(2)}) async-start(bf16[16,128,512]{2,1,0:T(8,128)(2,1)} %copy.165), calls=%async_computation | async-start | bytes 4194304 | tf_op jit(solution)/shard_map/all_to_all | solution.py:135
  74.8 11.4 %copy-start.8 = (s32[32,8]{0,1:T(8,128)S(1)}, s32[32,8]{0,1:T(8,128)}, u32[]{:S(2)}) copy-start(s32[32,8]{0,1:T(8,128)} %param.18) | copy-start | bytes 3076
  74.8 93.3 %reduce-scatter.3.cloned.1.call-start = ((), (), s32[]{:S(2)}) async-start(), calls=%async_computation.5 | async-start | bytes 1572864 | tf_op jit(solution)/shard_map/reduce_scatter | solution.py:148
  76.6 21.1 %collective-permute-start = (bf16[128,512]{1,0:T(8,128)(2,1)}, bf16[128,512]{1,0:T(8,128)(2,1)}, u32[]{:S(2)}, u32[]{:S(2)}) collective-permute-start(bf16[128,512]{1,0:T(8,128)(2,1)} %get-tuple-element.22), channel_id=1, source_target_pairs={{0,2},{2,4},{4,6},{6,8},{8,10},{10,12},{12,14},{14,16},{16,18},{18... | collective-permute-start | bytes 393224 | tf_op jit(solution)/shard_map/ppermute | solution.py:30
  80.2 20.6 %collective-permute-start.1 = (bf16[128,512]{1,0:T(8,128)(2,1)}, bf16[128,512]{1,0:T(8,128)(2,1)}, u32[]{:S(2)}, u32[]{:S(2)}) collective-permute-start(bf16[128,512]{1,0:T(8,128)(2,1)} %get-tuple-element.20), channel_id=1, source_target_pairs={{0,2},{2,4},{4,6},{6,8},{8,10},{10,12},{12,14},{14,16},{16,18},{18... | collective-permute-start | bytes 393224 | tf_op jit(solution)/shard_map/ppermute | solution.py:30
  119.4 2.0 copy-start.6
  122.7 1.4 copy-start.1
  124.1 0.7 copy-start.9
  124.1 1.0 copy-start.3
  124.1 1.2 copy-start.4
  125.8 1.7 copy-start.7
  125.8 42.3 %copy-start.5 = (bf16[256,1024]{1,0:T(8,128)(2,1)S(1)}, bf16[256,1024]{1,0:T(8,128)(2,1)}, u32[]{:S(2)}) copy-start(bf16[256,1024]{1,0:T(8,128)(2,1)} %param.12) | copy-start | bytes 1572868
  127.5 48.6 %copy-start.10 = (f32[512]{0:T(512)S(1)}, f32[512]{0:T(512)}, u32[]{:S(2)}) copy-start(f32[512]{0:T(512)} %param.20) | copy-start | bytes 6148
  170.4 15.7 %all-to-all-start.2 = ((bf16[2,128,512]{2,0,1:T(2,128)(2,1)}), bf16[2,128,512]{2,0,1:T(2,128)(2,1)S(1)}, u32[]{:S(2)}, u32[]{:S(2)}) async-start(bf16[2,128,512]{2,0,1:T(2,128)(2,1)} %copy.182), calls=%async_computation.3 | async-start | bytes 524288 | tf_op jit(solution)/shard_map/all_to_all | solution.py:168
  176.0 69.3 %reduce-scatter.5.cloned.1.call-start = ((), (), s32[]{:S(2)}) async-start(), calls=%async_computation.6 | async-start | bytes 1572864 | tf_op jit(solution)/shard_map/reduce_scatter | solution.py:179
  187.7 32.5 %copy-start.12 = (f32[1024]{0:T(1024)S(1)}, f32[1024]{0:T(1024)}, u32[]{:S(2)}) copy-start(f32[1024]{0:T(1024)} %param.21) | copy-start | bytes 12292
  187.7 5.4 %collective-permute-start.2 = (bf16[2,8,512]{2,1,0:T(8,128)(2,1)S(1)}, bf16[2,8,512]{2,1,0:T(8,128)(2,1)S(1)}, u32[]{:S(2)}, u32[]{:S(2)}) collective-permute-start(bf16[2,8,512]{2,1,0:T(8,128)(2,1)S(1)} %get-tuple-element.19), channel_id=1, source_target_pairs={{0,30},{2,0},{4,2},{6,4},{8,6},{10,8},{12,10},{14,12},{16,14},{18,... | collective-permute-start | bytes 49160 | tf_op jit(solution)/shard_map/ppermute | solution.py:18
  189.2 5.6 %collective-permute-start.3 = (bf16[2,8,512]{2,1,0:T(8,128)(2,1)S(1)}, bf16[2,8,512]{2,1,0:T(8,128)(2,1)S(1)}, u32[]{:S(2)}, u32[]{:S(2)}) collective-permute-start(bf16[2,8,512]{2,1,0:T(8,128)(2,1)S(1)} %get-tuple-element.18), channel_id=1, source_target_pairs={{0,28},{2,30},{4,0},{6,2},{8,4},{10,6},{12,8},{14,10},{16,12},{18,... | collective-permute-start | bytes 49160 | tf_op jit(solution)/shard_map/ppermute | solution.py:18
  190.2 4.8 %collective-permute-start.4 = (bf16[2,8,512]{2,1,0:T(8,128)(2,1)S(1)}, bf16[2,8,512]{2,1,0:T(8,128)(2,1)S(1)}, u32[]{:S(2)}, u32[]{:S(2)}) collective-permute-start(bf16[2,8,512]{2,1,0:T(8,128)(2,1)S(1)} %get-tuple-element.17), channel_id=1, source_target_pairs={{0,26},{2,28},{4,30},{6,0},{8,2},{10,4},{12,6},{14,8},{16,10},{18,... | collective-permute-start | bytes 49160 | tf_op jit(solution)/shard_map/ppermute | solution.py:18
  190.2 6.9 %collective-permute-start.5 = (bf16[2,8,512]{2,1,0:T(8,128)(2,1)S(1)}, bf16[2,8,512]{2,1,0:T(8,128)(2,1)S(1)}, u32[]{:S(2)}, u32[]{:S(2)}) collective-permute-start(bf16[2,8,512]{2,1,0:T(8,128)(2,1)S(1)} %get-tuple-element.16), channel_id=1, source_target_pairs={{0,24},{2,26},{4,28},{6,30},{8,0},{10,2},{12,4},{14,6},{16,8},{18,... | collective-permute-start | bytes 49160 | tf_op jit(solution)/shard_map/ppermute | solution.py:18
  191.1 8.3 %collective-permute-start.6 = (bf16[2,8,512]{2,1,0:T(8,128)(2,1)S(1)}, bf16[2,8,512]{2,1,0:T(8,128)(2,1)S(1)}, u32[]{:S(2)}, u32[]{:S(2)}) collective-permute-start(bf16[2,8,512]{2,1,0:T(8,128)(2,1)S(1)} %get-tuple-element.15), channel_id=1, source_target_pairs={{0,22},{2,24},{4,26},{6,28},{8,30},{10,0},{12,2},{14,4},{16,6},{18... | collective-permute-start | bytes 49160 | tf_op jit(solution)/shard_map/ppermute | solution.py:18
  193.1 7.9 %collective-permute-start.7 = (bf16[2,8,512]{2,1,0:T(8,128)(2,1)S(1)}, bf16[2,8,512]{2,1,0:T(8,128)(2,1)S(1)}, u32[]{:S(2)}, u32[]{:S(2)}) collective-permute-start(bf16[2,8,512]{2,1,0:T(8,128)(2,1)S(1)} %get-tuple-element.14), channel_id=1, source_target_pairs={{0,20},{2,22},{4,24},{6,26},{8,28},{10,30},{12,0},{14,2},{16,4},{1... | collective-permute-start | bytes 49160 | tf_op jit(solution)/shard_map/ppermute | solution.py:18
  194.7 6.3 %collective-permute-start.8 = (bf16[2,8,512]{2,1,0:T(8,128)(2,1)S(1)}, bf16[2,8,512]{2,1,0:T(8,128)(2,1)S(1)}, u32[]{:S(2)}, u32[]{:S(2)}) collective-permute-start(bf16[2,8,512]{2,1,0:T(8,128)(2,1)S(1)} %get-tuple-element.13), channel_id=1, source_target_pairs={{0,18},{2,20},{4,22},{6,24},{8,26},{10,28},{12,30},{14,0},{16,2},{... | collective-permute-start | bytes 49160 | tf_op jit(solution)/shard_map/ppermute | solution.py:18
  195.0 8.2 %collective-permute-start.9 = (bf16[2,8,512]{2,1,0:T(8,128)(2,1)S(1)}, bf16[2,8,512]{2,1,0:T(8,128)(2,1)S(1)}, u32[]{:S(2)}, u32[]{:S(2)}) collective-permute-start(bf16[2,8,512]{2,1,0:T(8,128)(2,1)S(1)} %get-tuple-element.12), channel_id=1, source_target_pairs={{0,16},{2,18},{4,20},{6,22},{8,24},{10,26},{12,28},{14,30},{16,0},... | collective-permute-start | bytes 49160 | tf_op jit(solution)/shard_map/ppermute | solution.py:18
  197.1 8.2 %collective-permute-start.10 = (bf16[2,8,512]{2,1,0:T(8,128)(2,1)S(1)}, bf16[2,8,512]{2,1,0:T(8,128)(2,1)S(1)}, u32[]{:S(2)}, u32[]{:S(2)}) collective-permute-start(bf16[2,8,512]{2,1,0:T(8,128)(2,1)S(1)} %get-tuple-element.11), channel_id=1, source_target_pairs={{0,14},{2,16},{4,18},{6,20},{8,22},{10,24},{12,26},{14,28},{16,30}... | collective-permute-start | bytes 49160 | tf_op jit(solution)/shard_map/ppermute | solution.py:18
  199.4 7.1 %collective-permute-start.11 = (bf16[2,8,512]{2,1,0:T(8,128)(2,1)S(1)}, bf16[2,8,512]{2,1,0:T(8,128)(2,1)S(1)}, u32[]{:S(2)}, u32[]{:S(2)}) collective-permute-start(bf16[2,8,512]{2,1,0:T(8,128)(2,1)S(1)} %get-tuple-element.10), channel_id=1, source_target_pairs={{0,12},{2,14},{4,16},{6,18},{8,20},{10,22},{12,24},{14,26},{16,28}... | collective-permute-start | bytes 49160 | tf_op jit(solution)/shard_map/ppermute | solution.py:18
  201.0 5.6 %collective-permute-start.12 = (bf16[2,8,512]{2,1,0:T(8,128)(2,1)S(1)}, bf16[2,8,512]{2,1,0:T(8,128)(2,1)S(1)}, u32[]{:S(2)}, u32[]{:S(2)}) collective-permute-start(bf16[2,8,512]{2,1,0:T(8,128)(2,1)S(1)} %get-tuple-element.9), channel_id=1, source_target_pairs={{0,10},{2,12},{4,14},{6,16},{8,18},{10,20},{12,22},{14,24},{16,26}... | collective-permute-start | bytes 49160 | tf_op jit(solution)/shard_map/ppermute | solution.py:18
  201.0 5.6 %collective-permute-start.13 = (bf16[2,8,512]{2,1,0:T(8,128)(2,1)S(1)}, bf16[2,8,512]{2,1,0:T(8,128)(2,1)S(1)}, u32[]{:S(2)}, u32[]{:S(2)}) collective-permute-start(bf16[2,8,512]{2,1,0:T(8,128)(2,1)S(1)} %get-tuple-element.8), channel_id=1, source_target_pairs={{0,8},{2,10},{4,12},{6,14},{8,16},{10,18},{12,20},{14,22},{16,24},... | collective-permute-start | bytes 49160 | tf_op jit(solution)/shard_map/ppermute | solution.py:18
  203.3 5.2 %collective-permute-start.14 = (bf16[2,8,512]{2,1,0:T(8,128)(2,1)S(1)}, bf16[2,8,512]{2,1,0:T(8,128)(2,1)S(1)}, u32[]{:S(2)}, u32[]{:S(2)}) collective-permute-start(bf16[2,8,512]{2,1,0:T(8,128)(2,1)S(1)} %get-tuple-element.7), channel_id=1, source_target_pairs={{0,6},{2,8},{4,10},{6,12},{8,14},{10,16},{12,18},{14,20},{16,22},{... | collective-permute-start | bytes 49160 | tf_op jit(solution)/shard_map/ppermute | solution.py:18
  205.3 6.4 %collective-permute-start.15 = (bf16[2,8,512]{2,1,0:T(8,128)(2,1)S(1)}, bf16[2,8,512]{2,1,0:T(8,128)(2,1)S(1)}, u32[]{:S(2)}, u32[]{:S(2)}) collective-permute-start(bf16[2,8,512]{2,1,0:T(8,128)(2,1)S(1)} %get-tuple-element.6), channel_id=1, source_target_pairs={{0,4},{2,6},{4,8},{6,10},{8,12},{10,14},{12,16},{14,18},{16,20},{1... | collective-permute-start | bytes 49160 | tf_op jit(solution)/shard_map/ppermute | solution.py:18
  206.6 5.9 %collective-permute-start.16 = (bf16[2,8,512]{2,1,0:T(8,128)(2,1)S(1)}, bf16[2,8,512]{2,1,0:T(8,128)(2,1)S(1)}, u32[]{:S(2)}, u32[]{:S(2)}) collective-permute-start(bf16[2,8,512]{2,1,0:T(8,128)(2,1)S(1)} %get-tuple-element.5), channel_id=1, source_target_pairs={{0,2},{2,4},{4,6},{6,8},{8,10},{10,12},{12,14},{14,16},{16,18},{18... | collective-permute-start | bytes 49160 | tf_op jit(solution)/shard_map/ppermute | solution.py:18
Sparse Core Ops, SparseCore 0:
  127.6 40.4 reduce-scatter.2
  227.5 17.7 reduce-scatter.4
